TPU v7x, 32 devices: a whole 2x2x4 slice. The times are simulated.
32 devices in a mesh: groups: 1, leaf: 32 (over z, y, x, core).
Axes of the slice: x: 2, y: 2, z: 4, core: 2. Of those that a mesh axis runs over, the one named last changes fastest.
Arguments:
- krylov_basis: float32 [8, 64, 131072], P(None, None, ('groups', 'leaf')), may hold values from -6 to 6
- geometry: float32 [7, 131072], P(None, ('groups', 'leaf')), may hold values from -1 to 1
- near_leaf: int32 [512, 9], P(('groups', 'leaf')), may hold values from 0 to 511, as said below
- far_dev: int32 [512, 16], P(('groups', 'leaf')), may hold values from 0 to 31, all different within a row; in each aligned block of 16 rows (0 to 15, 16 to 31, ...) at most 16 rows name the same one
- far_local: int32 [512, 16], P(('groups', 'leaf')), may hold values from 0 to 15
- ubases: bfloat16 [512, 64, 256], P(('groups', 'leaf')), may hold values from -0.375 to 0.375
- vbases: bfloat16 [512, 64, 256], P(('groups', 'leaf')), may hold values from -0.75 to 0.75
- coupling: bfloat16 [512, 64, 1024], P(('groups', 'leaf')), may hold values from -0.1875 to 0.1875
Outputs:
- hessen: float32 [9, 64], P('groups')
- next_vector: float32 [64, 131072], P(None, ('groups', 'leaf'))
Inputs may be any that keep to these rules, and one draw needn't show every extreme that they name: `near_leaf`: row i starts with i itself, then max(i - 16, 0) and min(i + 16, 511); every entry lies within 16 of i. `far_dev`: the 16 entries of a row differ; over the rows of one device each device number appears at most 16 times.
All inputs are finite; a program needn't handle non-finite values.
Results may differ from a plain program's by a relative error of at most 0.0041.
Values may be sent and summed in bfloat16 or wider, within the bound.
A program may use at most 128 MiB of HBM per device.

v0:
```python
import math

import jax
import jax.numpy as jnp
from jax import lax
from jax.sharding import PartitionSpec as P

SOFTENING = 0.01
FOUR_PI = 4.0 * math.pi
EPSILON = 1e-06


def padded(shard, sides, width):
    for axis, dim in sides:
        size, length = (lax.axis_size(axis), shard.shape[dim])
        up = [(i, (i + 1) % size) for i in range(size - 1)]
        down = [(j, i) for i, j in up]
        last = lax.slice_in_dim(shard, length - width, length, axis=dim)
        first = lax.slice_in_dim(shard, 0, width, axis=dim)
        before = lax.ppermute(last, axis, up)
        after = lax.ppermute(first, axis, down)
        shard = jnp.concatenate([before, shard, after], axis=dim)
    return shard


def pair_kernel(target, source):
    delta_x = target[0][:, None] - source[0][None, :]
    delta_y = target[1][:, None] - source[1][None, :]
    delta_z = target[2][:, None] - source[2][None, :]
    dist_sq = delta_x * delta_x + delta_y * delta_y + delta_z * delta_z + SOFTENING
    numerator = (
        source[3][None, :] * delta_x + source[4][None, :] * delta_y + source[5][None, :] * delta_z
    )
    return source[6][None, :] * numerator / (FOUR_PI * dist_sq * jnp.sqrt(dist_sq))


def shards(krylov_basis, geometry, near_leaf, far_dev, far_local, ubases, vbases, coupling):
    own_leaves = near_leaf.shape[0]
    rank_size = ubases.shape[1]
    leaf_size = ubases.shape[2]
    columns = krylov_basis.shape[1]
    krylov_len = krylov_basis.shape[0]
    far_count = far_dev.shape[1]
    peers = lax.axis_size("leaf")
    position = lax.axis_index("leaf")
    npts_all = own_leaves * leaf_size * peers
    q_last = krylov_basis[krylov_len - 1]
    density_bf = q_last.astype(jnp.bfloat16)
    sig_leaf = density_bf.reshape(columns, own_leaves, leaf_size).transpose(1, 0, 2)
    multipole = jnp.einsum(
        "irb,ipb->irp", sig_leaf, ubases, preferred_element_type=jnp.float32
    ).astype(jnp.bfloat16)
    flat_multi = multipole.reshape(own_leaves, columns * rank_size)
    flat_dev = far_dev.reshape(-1)
    flat_loc = far_local.reshape(-1)
    everything = lax.all_gather(flat_multi, "leaf", axis=0, tiled=True)
    fetched = everything[flat_dev * own_leaves + flat_loc]
    fetched = fetched.reshape(own_leaves, far_count, columns, rank_size)
    coupled = coupling.reshape(own_leaves, rank_size, far_count, rank_size)
    local_exp = jnp.einsum(
        "ikrq,ipkq->irp", fetched, coupled, preferred_element_type=jnp.float32
    ).astype(jnp.bfloat16)
    far_part = jnp.einsum("irp,ipa->ira", local_exp, vbases, preferred_element_type=jnp.float32)
    dens_halo = padded(density_bf, (("leaf", 1),), own_leaves * leaf_size)
    geo_halo = padded(geometry, (("leaf", 1),), own_leaves * leaf_size)
    dens_leaf = dens_halo.reshape(columns, 3 * own_leaves, leaf_size).transpose(1, 0, 2)
    geo_leaf = geo_halo.reshape(7, 3 * own_leaves, leaf_size).transpose(1, 0, 2)
    halo_start = position * own_leaves - own_leaves
    near_local = near_leaf - halo_start

    def one_leaf(index_leaf):
        neighbours = near_local[index_leaf]
        blocks = jax.vmap(pair_kernel, in_axes=(None, 0))(
            geo_leaf[index_leaf + own_leaves], geo_leaf[neighbours]
        )
        blocks = blocks.astype(jnp.bfloat16)
        return jnp.einsum(
            "jrb,jab->ra", dens_leaf[neighbours], blocks, preferred_element_type=jnp.float32
        )

    near_part = lax.map(one_leaf, jnp.arange(own_leaves, dtype=jnp.int32))
    applied = (near_part + far_part).transpose(1, 0, 2).reshape(columns, own_leaves * leaf_size)
    imaged = 0.5 * q_last + applied
    partial_value = jnp.einsum("krn,rn->kr", krylov_basis, imaged, precision=lax.Precision.HIGHEST)
    coeffs = lax.psum(partial_value, "leaf") / npts_all
    orthogonal = imaged - jnp.einsum(
        "kr,krn->rn", coeffs, krylov_basis, precision=lax.Precision.HIGHEST
    )
    squares = lax.psum(jnp.sum(orthogonal * orthogonal, axis=1), "leaf")
    norm_rms = jnp.sqrt(squares / npts_all + EPSILON)
    hessen = jnp.concatenate([coeffs, norm_rms[None, :]], axis=0)
    return (hessen, orthogonal / norm_rms[:, None])


def solution(mesh):
    in_specs = (
        P(None, None, ("groups", "leaf")),
        P(None, ("groups", "leaf")),
        P(("groups", "leaf"), None),
        P(("groups", "leaf"), None),
        P(("groups", "leaf"), None),
        P(("groups", "leaf"), None, None),
        P(("groups", "leaf"), None, None),
        P(("groups", "leaf"), None, None),
    )
    out_specs = (P("groups", None), P(None, ("groups", "leaf")))
    return jax.shard_map(shards, mesh=mesh, in_specs=in_specs, out_specs=out_specs, check_vma=False)
```

profile of v0, /device:TPU:0, one launch (start us, length us, event | category | flops | bytes accessed | tf_op | source)
XLA Modules:
  0.0 309.3 jit_solution(799159096818147209)
XLA Ops:
  13.8 6.6 %collective-permute-start = (bf16[64,4096]{1,0:T(8,128)(2,1)S(1)}, bf16[64,4096]{1,0:T(8,128)(2,1)}, u32[]{:S(2)}, u32[]{:S(2)}) collective-permute-start(bf16[64,4096]{1,0:T(8,128)(2,1)S(1)} %slice_bitcast_fusion), channel_id=1, source_target_pairs={{0,1},{1,2},{2,3},{3,4},{4,5},{5,6},{6,7},{7,8},{8,9},{9,10},{10,1... | collective-permute-start | bytes 1572872 | tf_op jit(solution)/shard_map/ppermute | solution.py:20
  23.9 3.2 %copy.21 = bf16[16,64,1024]{1,2,0:T(8,128)(2,1)} copy(bf16[16,64,1024]{2,1,0:T(8,128)(2,1)S(1)} %copy-done.1) | data formatting | bytes 4194304 | tf_op jit(solution)/shard_map/reshape | solution.py:59
  30.3 123.3 %while.12 = (s32[]{:T(128)}, f32[16,64,256]{2,1,0:T(8,128)}, s32[16]{0:T(128)S(1)}, s32[16,9]{1,0:T(8,128)S(1)}, bf16[48,64,256]{2,1,0:T(8,128)(2,1)S(1)}, /*ind...) while((s32[]{:T(128)}, f32[16,64,256]{2,1,0:T(8,128)}, ...), condition=%wide.region_1.2_spmd, body=%wide.region_0.1_spmd.sunk | while | flops 86705184 | bytes 1415597 | solution.py:81
  35.1 3.0 fusion.48
  42.8 3.0 fusion.48
  50.5 3.0 fusion.48
  58.2 3.0 fusion.48
  65.9 3.0 fusion.48
  73.6 3.0 fusion.48
  81.3 3.0 fusion.48
  89.0 3.0 fusion.48
  96.7 3.0 fusion.48
  104.4 3.0 fusion.48
  119.9 3.0 fusion.48
  127.6 3.0 fusion.48
  135.3 3.0 fusion.48
  153.7 6.6 %gather_fusion.2 = bf16[256,4096]{1,0:T(8,128)(2,1)S(1)} fusion(bf16[512,4096]{1,0:T(8,128)(2,1)} %all-gather.2.cloned.1.call-done, s32[1024]{0:T(1024)S(1)} %pad_clamp_fusion.1), kind=kCustom, calls=%fused_computation.2 | custom fusion | bytes 4195328 | tf_op jit(solution)/shard_map/gather | solution.py:57
  160.3 5.6 %reshape.110 = bf16[16,16,64,64]{3,2,1,0:T(8,128)(2,1)} reshape(bf16[256,4096]{1,0:T(8,128)(2,1)S(1)} %gather_fusion.2) | data formatting | bytes 4194304 | tf_op jit(solution)/shard_map/reshape | solution.py:58
  165.9 4.8 %fusion.24 = f32[16,8,8,256]{3,2,1,0:T(8,128)S(1)} fusion(f32[16,64,256]{2,1,0:T(8,128)} %get-tuple-element.79, bf16[16,64,256]{2,1,0:T(8,128)(2,1)S(1)} %copy-done, bf16[16,16,64,64]{3,2,1,0:T(8,128)(2,1)} %reshape.110, bf16[16,64,16,64]{1,3,2,0:T(8,128)(2,1)} %bitcast.119), kind=kOutput, calls=%fused_computation.44 | convolution fusion | flops 168099840 | bytes 6815744 | tf_op jit(solution)/shard_map/irp,ipa->ira/dot_general | solution.py:63
  172.1 24.6 %fusion.22 = f32[64,1,8]{2,1,0:T(1,128)S(1)} fusion(f32[8,64,4096]{2,1,0:T(8,128)} %param.10, f32[64,4096,1]{1,0,2:T(8,128)S(1)} %fusion.31), kind=kOutput, calls=%fused_computation.39 | convolution fusion | flops 25165824 | bytes 9439232 | tf_op jit(solution)/shard_map/krn,rn->kr/dot_general | solution.py:84
  196.8 44.5 %psum.14 = f32[8,64]{1,0:T(8,128)S(1)} all-reduce(f32[8,64]{1,0:T(8,128)S(1)} %bitcast.129), channel_id=1, replica_groups=mesh['groups'=1,'leaf'=32] {'leaf'}, use_global_device_ids=true, to_apply=%region_2.3 | all-reduce | flops 512 | bytes 4096 | tf_op jit(solution)/shard_map/psum | solution.py:85
  241.3 15.3 %fusion.20 = f32[64,1,4096]{2,1,0:T(1,128)S(1)} fusion(f32[8,64,1]{0,2,1:T(1,128)S(1)} %copy.19, f32[8,64,4096]{2,1,0:T(8,128)} %param.10), kind=kOutput, calls=%fused_computation.37 | convolution fusion | flops 25165824 | bytes 9439232 | tf_op jit(solution)/shard_map/kr,krn->rn/dot_general | solution.py:86
  258.7 40.2 %psum.15 = f32[64]{0:T(128)S(1)} all-reduce(f32[64]{0:T(128)S(1)} %multiply_reduce_fusion), channel_id=1, replica_groups=mesh['groups'=1,'leaf'=32] {'leaf'}, use_global_device_ids=true, to_apply=%region_4.5 | all-reduce | flops 64 | bytes 512 | tf_op jit(solution)/shard_map/psum | solution.py:89
  298.9 3.0 broadcast_divide_fusion
  (224 shorter events, 56.5 us)
Async XLA Ops:
  7.2 158.7 %copy-start = (bf16[16,64,256]{2,1,0:T(8,128)(2,1)S(1)}, bf16[16,64,256]{2,1,0:T(8,128)(2,1)}, u32[]{:S(2)}) copy-start(bf16[16,64,256]{2,1,0:T(8,128)(2,1)} %param.16) | copy-start | bytes 1572868
  7.2 15.9 %copy-start.4 = (s32[16,16]{1,0:T(8,128)S(1)}, s32[16,16]{1,0:T(8,128)}, u32[]{:S(2)}) copy-start(s32[16,16]{1,0:T(8,128)} %param.14) | copy-start | bytes 3076
  7.2 15.9 %copy-start.5 = (s32[16,16]{1,0:T(8,128)S(1)}, s32[16,16]{1,0:T(8,128)}, u32[]{:S(2)}) copy-start(s32[16,16]{1,0:T(8,128)} %param.13) | copy-start | bytes 3076
  7.2 16.7 %copy-start.1 = (bf16[16,64,1024]{2,1,0:T(8,128)(2,1)S(1)}, bf16[16,64,1024]{2,1,0:T(8,128)(2,1)}, u32[]{:S(2)}) copy-start(bf16[16,64,1024]{2,1,0:T(8,128)(2,1)} %param.17) | copy-start | bytes 6291460
  7.2 146.5 %all-gather.2.cloned.1.call-start = ((), (), s32[]{:S(2)}) async-start(), calls=%async_computation | async-start | bytes 4325376 | tf_op jit(solution)/shard_map/all_gather | solution.py:56
  7.3 14.5 %copy-start.2 = (bf16[16,64,256]{2,1,0:T(8,128)(2,1)S(1)}, bf16[16,64,256]{2,1,0:T(8,128)(2,1)}, u32[]{:S(2)}) copy-start(bf16[16,64,256]{2,1,0:T(8,128)(2,1)} %param.15) | copy-start | bytes 1572868
  7.3 19.8 %collective-permute-start.2 = (f32[7,4096]{1,0:T(8,128)}, f32[7,4096]{1,0:T(8,128)S(1)}, u32[]{:S(2)}, u32[]{:S(2)}) collective-permute-start(f32[7,4096]{1,0:T(8,128)} %param.11), channel_id=1, source_target_pairs={{0,1},{1,2},{2,3},{3,4},{4,5},{5,6},{6,7},{7,8},{8,9},{9,10},{10,1... | collective-permute-start | bytes 344072 | tf_op jit(solution)/shard_map/ppermute | solution.py:20
  9.9 17.8 %collective-permute-start.3 = (f32[7,4096]{1,0:T(8,128)}, f32[7,4096]{1,0:T(8,128)}, u32[]{:S(2)}, u32[]{:S(2)}) collective-permute-start(f32[7,4096]{1,0:T(8,128)} %param.11), channel_id=1, source_target_pairs={{1,0},{2,1},{3,2},{4,3},{5,4},{6,5},{7,6},{8,7},{9,8},{10,9},{11,1... | collective-permute-start | bytes 344072 | tf_op jit(solution)/shard_map/ppermute | solution.py:21
  12.5 16.3 %collective-permute-start.1 = (bf16[64,4096]{1,0:T(8,128)(2,1)S(1)}, bf16[64,4096]{1,0:T(8,128)(2,1)}, u32[]{:S(2)}, u32[]{:S(2)}) collective-permute-start(bf16[64,4096]{1,0:T(8,128)(2,1)S(1)} %slice_bitcast_fusion), channel_id=1, source_target_pairs={{1,0},{2,1},{3,2},{4,3},{5,4},{6,5},{7,6},{8,7},{9,8},{10,9},{11,1... | collective-permute-start | bytes 1572872 | tf_op jit(solution)/shard_map/ppermute | solution.py:21
  13.8 15.0 %collective-permute-start = (bf16[64,4096]{1,0:T(8,128)(2,1)S(1)}, bf16[64,4096]{1,0:T(8,128)(2,1)}, u32[]{:S(2)}, u32[]{:S(2)}) collective-permute-start(bf16[64,4096]{1,0:T(8,128)(2,1)S(1)} %slice_bitcast_fusion), channel_id=1, source_target_pairs={{0,1},{1,2},{2,3},{3,4},{4,5},{5,6},{6,7},{7,8},{8,9},{9,10},{10,1... | collective-permute-start | bytes 1572872 | tf_op jit(solution)/shard_map/ppermute | solution.py:20
  27.1 0.7 copy-start.3
Sparse Core Ops, SparseCore 0:
  23.2 64.6 all-gather.1
where the time goes:
time: 311 us; the launch traced here: 309 us
  matrix products  92.7 us (30%)
  blocking collectives  84.6 us (27%)
  local copies, waits for them, and re-layouts  49.9 us (16%)
  loops' own time  45.5 us (15%)
  between operations  14.2 us (5%)
  starting transfers between devices  11.9 us (4%)
  other arithmetic  10.4 us (3%)
    dot_general x16, matrix products, one_leaf(): jnp.einsum('jrb,jab->ra', dens_leaf[neighbours], blocks, preferred_elemen...  47.7 us
    another operation x1, loops' own time, shards(): near_part = lax.map(one_leaf, jnp.arange(own_leaves, dtype=jnp.int32))  45.5 us
    psum x1, blocking collectives, shards(): coeffs = lax.psum(partial_value, 'leaf') / npts_all  44.5 us
    psum x1, blocking collectives, shards(): squares = lax.psum(jnp.sum(orthogonal * orthogonal, axis=1), 'leaf')  40.2 us
    dot_general x1, matrix products, shards(): jnp.einsum('krn,rn->kr', krylov_basis, imaged, precision=lax.Precision.HI...  24.6 us
    dot_general x1, matrix products, shards(): jnp.einsum('kr,krn->rn', coeffs, krylov_basis, precision=lax.Precision.HI...  15.3 us
    dynamic_slice x16, local copies, waits for them, and re-layouts, shards(): near_part = lax.map(one_leaf, jnp.arange(own_leaves, dtype=jnp.int32))  10.6 us
    ppermute x2, starting transfers between devices, padded(): before = lax.ppermute(last, axis, up)  9.23 us
  transfers between devices with their start and end apart: 5, of which 0 were waited for; matrix products, arithmetic and copies ran while one was open for 29% of the time, Pallas kernels for 0%

commit v1 on v0

v1 whole, which is shorter than its diff:
```python
import functools
import math

import jax
import jax.numpy as jnp
import numpy as np
from jax import lax
from jax.experimental import pallas as pl
from jax.experimental.pallas import tpu as pltpu
from jax.sharding import PartitionSpec as P

SOFTENING = 0.01
FOUR_PI = 4.0 * math.pi
EPSILON = 1e-06
MESH = pl.DeviceIdType.MESH
GROUP = 8
FEATURES = 48
F32, BF16 = jnp.float32, jnp.bfloat16


def selections():
    src = np.zeros((32, FEATURES), np.float32)
    tgt = np.zeros((2, FEATURES, 32), np.float32)
    one, f = 24, 0
    for ps, pt in ((0, 0), (0, 1), (1, 0), (1, 1), (0, 2), (2, 0)):
        for c in range(3):
            src[8 * ps + c, f], tgt[0, f, 8 * pt + c] = -2.0, 1.0
            f += 1
            src[8 * ps + 4 + c, f], tgt[1, f, 8 * pt + c] = 1.0, 1.0
            f += 1
    for p in range(3):
        src[8 * p + 3, f], tgt[0, f, one] = 1.0, 1.0
        src[one, f + 1], tgt[0, f + 1, 8 * p + 3] = 1.0, 1.0
        src[8 * p + 7, f + 2], tgt[1, f + 2, one] = 1.0, 1.0
        f += 3
    return src.astype(BF16), tgt.astype(BF16)


def pieces(q):
    a = q.astype(BF16).astype(F32)
    b = (q - a).astype(BF16).astype(F32)
    c = ((q - a) - b).astype(BF16).astype(F32)
    return jnp.concatenate([a, b, c, jnp.ones_like(a)], axis=0)


def dot(a, b, dims=((1,), (0,))):
    return lax.dot_general(a, b, (dims, ((), ())), preferred_element_type=F32)


def kernel(
    n, leaves, npts,
    near_idx, far_idx, q_hbm, src_sel, tgt_sel, krylov_hbm, u_hbm, v_hbm, c_hbm,
    hess_ref, out_ref,
    kry, ub, vb, cp, qh, dens, feats, every, near, imaged, acc, square, red,
    in_sem, halo_send, halo_recv, ag_send, ag_recv, red_send, red_recv,
):
    me = lax.axis_index("leaf")
    bits = n.bit_length() - 1
    lines = n // GROUP
    low, high = lax.rem(me, GROUP), lax.div(me, GROUP)
    krylov_len = kry.shape[0]
    width = dens.shape[3]
    right, left = lax.rem(me + 1, n), lax.rem(me + n - 1, n)

    def group_peer(d):
        return high * GROUP + lax.rem(low + d, GROUP)

    def line_peer(d):
        return lax.rem(high + d, lines) * GROUP + low

    barrier = pltpu.get_barrier_semaphore()
    peers = [group_peer(d) for d in range(1, GROUP)] + [line_peer(d) for d in range(1, lines)] + [left, right]
    for peer in peers:
        pl.semaphore_signal(barrier, inc=1, device_id={"leaf": peer}, device_id_type=MESH)

    last = krylov_len - 1
    copies = [
        pltpu.make_async_copy(krylov_hbm.at[last], kry.at[last], in_sem.at[0]),
        pltpu.make_async_copy(q_hbm, qh.at[1], in_sem.at[1]),
        pltpu.make_async_copy(u_hbm, ub, in_sem.at[2]),
        pltpu.make_async_copy(c_hbm, cp, in_sem.at[3]),
        pltpu.make_async_copy(v_hbm, vb, in_sem.at[4]),
        pltpu.make_async_copy(krylov_hbm.at[pl.ds(0, last)], kry.at[pl.ds(0, last)], in_sem.at[5]),
    ]
    for copy in copies:
        copy.start()
    copies[0].wait()
    for i in range(leaves):
        dens[1, i] = kry[last, :, i * width:(i + 1) * width].astype(BF16)
    copies[1].wait()
    pl.semaphore_wait(barrier, len(peers))
    halos = []
    for t, (ref, peer, slot) in enumerate(((qh, right, 0), (qh, left, 2), (dens, right, 0), (dens, left, 2))):
        halos.append(pltpu.make_async_remote_copy(
            src_ref=ref.at[1], dst_ref=ref.at[slot], send_sem=halo_send.at[t], recv_sem=halo_recv.at[t],
            device_id={"leaf": peer}, device_id_type=MESH))
        halos[-1].start()

    slot = sum(lax.rem(lax.div(me, 1 << b), 2) * (1 << (bits - 1 - b)) for b in range(bits))
    copies[2].wait()

    @pl.loop(0, leaves)
    def _(i):
        m = dot(ub[i], dens[1, i], ((1,), (1,))).astype(BF16)
        half = m.shape[0] // 2
        every[slot, i] = jnp.concatenate([m[:half], m[half:]], axis=1)

    gathers = []
    for step in range(bits):
        bit, size = 1 << (bits - 1 - step), 1 << step
        peer = me + bit * (1 - 2 * lax.rem(lax.div(me, bit), 2))
        held = every.at[pl.ds(lax.div(slot, size) * size, size)]
        gathers.append(pltpu.make_async_remote_copy(
            src_ref=held, dst_ref=held, send_sem=ag_send.at[step], recv_sem=ag_recv.at[step],
            device_id={"leaf": peer}, device_id_type=MESH))
    gathers[0].start()

    def features(side):
        @pl.loop(0, leaves)
        def _(i):
            at = pl.ds(pl.multiple_of(i * width, width), width)
            parts = pieces(qh[side, :, at])
            feats[side * leaves + i] = dot(parts.T.astype(BF16), src_sel[...]).astype(BF16)

    features(1)
    for t in (0, 2, 1, 3):
        halos[t].wait()
    features(0)
    features(2)

    marks = [1 + (leaves - 3) * (step + 1) // bits for step in range(bits - 1)]

    @pl.loop(0, leaves)
    def _(i):
        for step in range(bits - 1):
            @pl.when(i == marks[step])
            def _():
                gathers[step].wait()
                gathers[step + 1].start()

        at = pl.ds(pl.multiple_of(i * width, width), width)
        parts = pieces(qh[1, :, at]).astype(BF16)
        weights = jnp.concatenate([dot(tgt_sel[0], parts), dot(tgt_sel[1], parts)], axis=1).astype(BF16)
        total = jnp.zeros(near.shape[1:], F32)
        for j in range(near_idx.shape[1]):
            leaf = near_idx[i, j]
            both = dot(feats[leaf], weights)
            root = lax.rsqrt(both[:, :width])
            block = (both[:, width:] * (root * root * root)).astype(BF16)
            total += dot(dens[lax.div(leaf, leaves), lax.rem(leaf, leaves)], block)
        near[i] = total

    for copy in copies[3:]:
        copy.wait()
    gathers[-1].wait()

    acc[...] = jnp.zeros_like(acc)

    @pl.loop(0, leaves)
    def _(i):
        at = pl.ds(pl.multiple_of(i * width, width), width)
        rows = []
        for k in range(far_idx.shape[1]):
            where = far_idx[i, k]
            m = every[lax.div(where, leaves), lax.rem(where, leaves)]
            half = m.shape[1] // 2
            rows += [m[:, :half], m[:, half:]]
        local = dot(cp[i], jnp.concatenate(rows, axis=0)).astype(BF16).astype(F32)
        far = dot(local.T.astype(BF16), vb[i])
        value = 0.5 * kry[last, :, at] + (near[i] + far)
        imaged[:, at] = value
        for k in range(krylov_len):
            prod = kry[k, :, at] * value
            acc[k] += sum(prod[:, s:s + 128] for s in range(0, width, 128))

    lane = lax.broadcasted_iota(jnp.int32, square.shape, 1)
    rows_r = imaged.shape[0]

    def to_rows(columns):
        square[...] = jnp.zeros_like(square)
        held = jnp.zeros((rows_r, 128), F32)
        for k, column in enumerate(columns):
            held = jnp.where(lane[:rows_r] == k, column, held)
        square[0:rows_r, :] = held
        return square[...].T[0:8]

    def all_sum(phase, block):
        for level, (count, mine, peer_of) in enumerate(((GROUP, low, group_peer), (lines, high, line_peer))):
            base = 2 * phase + level
            red[base, mine] = block
            sent = []
            for d in range(1, count):
                sent.append(pltpu.make_async_remote_copy(
                    src_ref=red.at[base, mine], dst_ref=red.at[base, mine],
                    send_sem=red_send.at[base, d], recv_sem=red_recv.at[base, d],
                    device_id={"leaf": peer_of(d)}, device_id_type=MESH))
                sent[-1].start()
            for copy in sent:
                copy.wait()
            block = red[base, 0]
            for d in range(1, count):
                block = block + red[base, d]
        return block

    def to_columns(block):
        square[...] = jnp.zeros_like(square)
        square[0:8, :] = block
        return square[...].T[0:rows_r]

    partial = to_rows([jnp.sum(acc[k], axis=1, keepdims=True) for k in range(krylov_len)])
    coeffs = all_sum(0, partial) * (1.0 / npts)
    hess_ref[0:krylov_len, :] = coeffs[0:krylov_len, 0:rows_r]
    lanes = to_columns(coeffs)
    factor = [jnp.sum(jnp.where(lane[:rows_r] == k, lanes, 0.0), axis=1, keepdims=True) for k in range(krylov_len)]
    for k in range(krylov_len):
        acc[k] = jnp.broadcast_to(factor[k], (rows_r, 128))
    near[0, :, 0:128] = jnp.zeros((rows_r, 128), F32)

    @pl.loop(0, leaves * width // 128)
    def _(i):
        at = pl.ds(pl.multiple_of(i * 128, 128), 128)
        value = imaged[:, at]
        shift = acc[0] * kry[0, :, at]
        for k in range(1, krylov_len):
            shift += acc[k] * kry[k, :, at]
        value = value - shift
        imaged[:, at] = value
        near[0, :, 0:128] += value * value

    squares = all_sum(1, to_rows([jnp.sum(near[0, :, 0:128], axis=1, keepdims=True)]))
    norm = jnp.sqrt(squares * (1.0 / npts) + EPSILON)
    hess_ref[krylov_len:krylov_len + 1, :] = norm[0:1, 0:rows_r]
    inverse = jnp.broadcast_to(1.0 / to_columns(norm)[:, 0:1], (rows_r, width))

    @pl.loop(0, leaves)
    def _(i):
        at = pl.ds(pl.multiple_of(i * width, width), width)
        out_ref[:, at] = imaged[:, at] * inverse


def shards(n, krylov_basis, geometry, near_leaf, far_dev, far_local, ubases, vbases, coupling):
    leaves, rank, width = ubases.shape
    krylov_len, columns, points = krylov_basis.shape
    position = lax.axis_index("leaf")
    bits = n.bit_length() - 1
    near_idx = near_leaf - position * leaves + leaves
    reverse = sum(((far_dev >> b) & 1) << (bits - 1 - b) for b in range(bits))
    far_idx = reverse * leaves + far_local
    x, normal, weight = geometry[0:3], geometry[3:6], geometry[6:7]
    moment = weight * normal * (1.0 / FOUR_PI)
    quantities = jnp.concatenate(
        [
            x,
            jnp.sum(x * x, axis=0, keepdims=True) + 0.5 * SOFTENING,
            moment,
            -jnp.sum(moment * x, axis=0, keepdims=True),
        ],
        axis=0,
    )
    src_sel, tgt_sel = selections()
    lines = n // GROUP
    smem, vmem, hbm = (pl.BlockSpec(memory_space=s) for s in (pltpu.SMEM, pltpu.VMEM, pl.ANY))
    return pl.pallas_call(
        functools.partial(kernel, n, leaves, n * points),
        out_shape=(
            jax.ShapeDtypeStruct((krylov_len + 1, columns), F32),
            jax.ShapeDtypeStruct((columns, points), F32),
        ),
        in_specs=[smem, smem, hbm, vmem, vmem, hbm, hbm, hbm, hbm],
        out_specs=(vmem, vmem),
        scratch_shapes=[
            pltpu.VMEM(krylov_basis.shape, F32),
            pltpu.VMEM(ubases.shape, BF16),
            pltpu.VMEM(vbases.shape, BF16),
            pltpu.VMEM(coupling.shape, BF16),
            pltpu.VMEM((3, 8, points), F32),
            pltpu.VMEM((3, leaves, columns, width), BF16),
            pltpu.VMEM((3 * leaves, width, FEATURES), BF16),
            pltpu.VMEM((n, leaves, rank // 2, 2 * columns), BF16),
            pltpu.VMEM((leaves, columns, width), F32),
            pltpu.VMEM((columns, points), F32),
            pltpu.VMEM((krylov_len, columns, 128), F32),
            pltpu.VMEM((128, 128), F32),
            pltpu.VMEM((4, max(GROUP, lines), 8, 128), F32),
            pltpu.SemaphoreType.DMA((6,)),
            pltpu.SemaphoreType.DMA((4,)),
            pltpu.SemaphoreType.DMA((4,)),
            pltpu.SemaphoreType.DMA((bits,)),
            pltpu.SemaphoreType.DMA((bits,)),
            pltpu.SemaphoreType.DMA((4, max(GROUP, lines))),
            pltpu.SemaphoreType.DMA((4, max(GROUP, lines))),
        ],
        compiler_params=pltpu.CompilerParams(
            collective_id=0, has_side_effects=True, vmem_limit_bytes=56 * 1024 * 1024
        ),
    )(near_idx, far_idx, quantities, jnp.asarray(src_sel), jnp.asarray(tgt_sel), krylov_basis, ubases, vbases, coupling)


def solution(mesh):
    in_specs = (
        P(None, None, ("groups", "leaf")),
        P(None, ("groups", "leaf")),
        P(("groups", "leaf"), None),
        P(("groups", "leaf"), None),
        P(("groups", "leaf"), None),
        P(("groups", "leaf"), None, None),
        P(("groups", "leaf"), None, None),
        P(("groups", "leaf"), None, None),
    )
    out_specs = (P("groups", None), P(None, ("groups", "leaf")))
    return jax.shard_map(
        functools.partial(shards, mesh.shape["leaf"]),
        mesh=mesh, in_specs=in_specs, out_specs=out_specs, check_vma=False,
    )
```

time: 311 us -> 124 us (0.40)
  Pallas kernels: 0 us -> 114 us
  matrix products: 92.7 us -> 0 us
  blocking collectives: 84.6 us -> 0 us
  loops' own time: 45.5 us -> 0 us
  local copies, waits for them, and re-layouts: 49.9 us -> 4.49 us
  between operations: 14.2 us -> 0.67 us
  starting transfers between devices: 11.9 us -> 0 us
  other arithmetic: 10.4 us -> 4.44 us
    pallas_call x0 -> x1, Pallas kernels: none -> 114 us  [shards(): pl.pallas_call(functools.partial(kernel, n, leaves, n * points), out_shap...]
    dot_general x20 -> x0, matrix products: 92.7 us -> none  [the longest x16 47.7 us: one_leaf(): jnp.einsum('jrb,jab->ra', dens_leaf[neighbours], blocks, preferred_elemen...]
    psum x2 -> x0, blocking collectives: 84.6 us -> none  [the longest x1 44.5 us: shards(): coeffs = lax.psum(partial_value, 'leaf') / npts_all]
    another operation x1 -> x0, loops' own time: 45.5 us -> none  [shards(): near_part = lax.map(one_leaf, jnp.arange(own_leaves, dtype=jnp.int32))]
    gather x33 -> x0, local copies, waits for them, and re-layouts: 24.6 us -> none  [the longest x16 9.05 us: one_leaf(): dens_leaf[neighbours]]
    ppermute x4 -> x0, starting transfers between devices: 11.8 us -> none  [the longest x2 9.23 us: padded(): before = lax.ppermute(last, axis, up)]
    dynamic_slice x16 -> x0, local copies, waits for them, and re-layouts: 10.6 us -> none  [shards(): near_part = lax.map(one_leaf, jnp.arange(own_leaves, dtype=jnp.int32))]
    reshape x5 -> x0, local copies, waits for them, and re-layouts: 9.95 us -> none  [the longest x1 5.56 us: shards(): fetched = fetched.reshape(own_leaves, far_count, columns, rank_size)]
  transfers between devices with their start and end apart: 5 -> 0, of which waited for: 0 -> 0; matrix products, arithmetic and copies ran while one was open for 29% -> 0% of each run, Pallas kernels for 0% -> 0%
where the time goes in v1:
time: 124 us; the launch traced here: 123 us
  Pallas kernels  114 us (92%)
  local copies, waits for them, and re-layouts  4.49 us (4%)
  other arithmetic  4.44 us (4%)
    pallas_call x1, Pallas kernels, shards(): pl.pallas_call(functools.partial(kernel, n, leaves, n * points), out_shap...  114 us
    unnamed x2, local copies, waits for them, and re-layouts  3.57 us

profile of v1, /device:TPU:0, one launch (start us, length us, event | category | flops | bytes accessed | tf_op | source)
XLA Modules:
  0.0 123.5 jit_solution(478925009436758174)
XLA Ops:
  0.6 1.3 %subtract_add_fusion.near_idx = s32[16,9]{1,0:T(8,128)} fusion(s32[16,9]{1,0:T(8,128)} %param.12, s32[]{:T(128)S(6)} %mul.31), kind=kLoop, calls=%fused_computation.6 | loop fusion | flops 288 | bytes 1156 | tf_op jit(solution)/shard_map/add | solution.py:246
  1.9 1.3 %multiply_add_fusion.far_idx = s32[16,16]{1,0:T(8,128)} fusion(s32[16,16]{1,0:T(8,128)} %param.14, s32[16,16]{1,0:T(8,128)} %param.13), kind=kLoop, calls=%fused_computation.5 | loop fusion | flops 5376 | bytes 3072 | tf_op jit(solution)/shard_map/add | solution.py:248
  3.2 0.9 slice.10
  4.2 1.1 multiply_reduce_fusion.1
  5.3 0.7 pad_maximum_fusion.q_hbm
  6.0 113.9 %shard_map.113 = (f32[9,64]{1,0:T(8,128)}, f32[64,4096]{1,0:T(8,128)}) custom-call(s32[16,9]{1,0:T(8,128)} %subtract_add_fusion.near_idx, s32[16,16]{1,0:T(8,128)} %multiply_add_fusion.far_idx, f32[8,4096]{1,0:T(8,128)} %pad_maximum_fusion.q_hbm, bf16[32,48]{1,0:T(8,128)(2,1)} %constant.10.clone.src_sel, bf16[2,48,32]{2,1,0:T(8,128)(2,1)} %constant.11.clone.tgt_sel, ...), custom_call_target="tpu_custom_call" | custom-call | tf_op jit(solution)/shard_map/pallas_call | solution.py:263
  119.9 1.3 %copy.14 = f32[9,64]{1,0:T(8,128)} copy(f32[9,64]{1,0:T(8,128)} %get-tuple-element.8) | data formatting | bytes 4608
  121.2 2.3 %copy.15 = f32[64,4096]{1,0:T(8,128)} copy(f32[64,4096]{1,0:T(8,128)} %get-tuple-element.9) | data formatting | bytes 2097152
  (2 shorter events, 0.0 us)

commit v2 on v1

v2 whole, which is shorter than its diff:
```python
import functools
import math

import jax
import jax.numpy as jnp
import numpy as np
from jax import lax
from jax.experimental import pallas as pl
from jax.experimental.pallas import tpu as pltpu
from jax.sharding import PartitionSpec as P

SOFTENING = 0.01
FOUR_PI = 4.0 * math.pi
EPSILON = 1e-06
MESH = pl.DeviceIdType.MESH
GROUP = 8
FEATURES = 48
MARKS = (4, 11)
F32, BF16 = jnp.float32, jnp.bfloat16


def selections():
    src = np.zeros((32, FEATURES), np.float32)
    tgt = np.zeros((2, FEATURES, 32), np.float32)
    one, f = 24, 0
    for ps, pt in ((0, 0), (0, 1), (1, 0), (1, 1), (0, 2), (2, 0)):
        for c in range(3):
            src[8 * ps + c, f], tgt[0, f, 8 * pt + c] = -2.0, 1.0
            f += 1
            src[8 * ps + 4 + c, f], tgt[1, f, 8 * pt + c] = 1.0, 1.0
            f += 1
    for p in range(3):
        src[8 * p + 3, f], tgt[0, f, one] = 1.0, 1.0
        src[one, f + 1], tgt[0, f + 1, 8 * p + 3] = 1.0, 1.0
        src[8 * p + 7, f + 2], tgt[1, f + 2, one] = 1.0, 1.0
        f += 3
    return src.astype(BF16), tgt.astype(BF16)


def pieces(q):
    a = q.astype(BF16).astype(F32)
    b = (q - a).astype(BF16).astype(F32)
    c = ((q - a) - b).astype(BF16).astype(F32)
    return jnp.concatenate([a, b, c, jnp.ones_like(a)], axis=0)


def dot(a, b, dims=((1,), (0,))):
    return lax.dot_general(a, b, (dims, ((), ())), preferred_element_type=F32)


def kernel(
    n, leaves, npts,
    near_ref, far_dev, far_local, slot_of, geo_ref, src_sel, tgt_sel, krylov_hbm, u_hbm, v_hbm, c_hbm,
    hess_ref, out_ref,
    kry, ub, vb, cp, qh, dens, feats, every, applied, grams, acc, square, red_g, red_p,
    in_sem, halo_send, halo_recv, ag_send, ag_recv, red_send, red_recv,
):
    me = lax.axis_index("leaf")
    bits = n.bit_length() - 1
    lines = n // GROUP
    low, high = lax.rem(me, GROUP), lax.div(me, GROUP)
    krylov_len, rows_r = kry.shape[0], kry.shape[1]
    last = krylov_len - 1
    width = dens.shape[3]
    right, left = lax.rem(me + 1, n), lax.rem(me + n - 1, n)
    pairs = [(k, m) for k in range(krylov_len) for m in range(k, krylov_len)]

    def remote(src, dst, peer, send, recv):
        return pltpu.make_async_remote_copy(
            src_ref=src, dst_ref=dst, send_sem=send, recv_sem=recv,
            device_id={"leaf": peer}, device_id_type=MESH)

    def group_peer(d):
        return high * GROUP + lax.rem(low + d, GROUP)

    def line_peer(d):
        return lax.rem(high + d, lines) * GROUP + low

    barrier = pltpu.get_barrier_semaphore()
    peers = [group_peer(d) for d in range(1, GROUP)] + [line_peer(d) for d in range(1, lines)] + [left, right]
    for peer in peers:
        pl.semaphore_signal(barrier, inc=1, device_id={"leaf": peer}, device_id_type=MESH)

    copies = [
        pltpu.make_async_copy(krylov_hbm.at[last], kry.at[last], in_sem.at[0]),
        pltpu.make_async_copy(u_hbm, ub, in_sem.at[1]),
        pltpu.make_async_copy(krylov_hbm.at[pl.ds(0, last)], kry.at[pl.ds(0, last)], in_sem.at[2]),
        pltpu.make_async_copy(c_hbm, cp, in_sem.at[3]),
        pltpu.make_async_copy(v_hbm, vb, in_sem.at[4]),
    ]
    for copy in copies:
        copy.start()

    geo = geo_ref[...]
    x, normal, weight = geo[0:3], geo[3:6], geo[6:7]
    moment = weight * normal * (1.0 / FOUR_PI)
    sq = x * x
    mx = moment * x
    qh[1] = jnp.concatenate(
        [
            x,
            sq[0:1] + sq[1:2] + sq[2:3] + 0.5 * SOFTENING,
            moment,
            -(mx[0:1] + mx[1:2] + mx[2:3]),
        ],
        axis=0,
    )

    copies[0].wait()
    for i in range(leaves):
        dens[1, i] = kry[last, :, i * width:(i + 1) * width].astype(BF16)
    pl.semaphore_wait(barrier, len(peers))
    halos = []
    for t, (ref, peer, slot) in enumerate(((qh, right, 0), (qh, left, 2), (dens, right, 0), (dens, left, 2))):
        halos.append(remote(ref.at[1], ref.at[slot], peer, halo_send.at[t], halo_recv.at[t]))
        halos[-1].start()

    slot = sum(lax.rem(lax.div(me, 1 << b), 2) * (1 << (bits - 1 - b)) for b in range(bits))
    copies[1].wait()

    @pl.loop(0, leaves, unroll=4)
    def _(i):
        m = dot(ub[i], dens[1, i], ((1,), (1,))).astype(BF16)
        half = m.shape[0] // 2
        every[slot, i] = jnp.concatenate([m[:half], m[half:]], axis=1)

    made = []

    def gather(first, count, leaf, peer):
        view = every.at[pl.ds(first, count), pl.ds(leaf[0], leaf[1])]
        made.append(remote(view, view, peer, ag_send.at[len(made)], ag_recv.at[len(made)]))
        return made[-1]

    def digit(b):
        return lax.rem(lax.div(me, 1 << b), 2)

    def across(b):
        return me + (1 << b) * (1 - 2 * digit(b))

    steps = bits - 3
    size = 1 << steps
    core, inner, outer = digit(0), digit(1), digit(2)

    def region(o, i):
        return (core * 4 + i * 2 + o) * size

    whole, front, back = (0, leaves), (0, leaves // 2), (leaves // 2, leaves // 2)
    highs = [
        gather(lax.div(slot, 1 << t) * (1 << t), 1 << t, whole, across(bits - 1 - t)) for t in range(steps)
    ]
    mine = region(outer, inner)
    first = [gather(mine, size, front, across(2)), gather(mine, size, back, across(1))]
    side0 = [gather(mine, size, whole, across(0))]
    second = [
        gather(region(0, inner), 2 * size, front, across(1)),
        gather(region(outer, 0), size, back, across(2)),
        gather(region(outer, 1), size, back, across(2)),
    ]
    side1 = [
        gather(region(1 - outer, inner), size, front, across(0)),
        gather(region(outer, 1 - inner), size, back, across(0)),
    ]
    side2 = [
        gather(region(0, 1 - inner), 2 * size, front, across(0)),
        gather(region(1 - outer, 0), size, back, across(0)),
        gather(region(1 - outer, 1), size, back, across(0)),
    ]

    def start(many):
        for copy in many:
            copy.start()

    def wait(many):
        for copy in many:
            copy.wait()

    highs[0].start()

    def features(side):
        @pl.loop(0, leaves, unroll=4)
        def _(i):
            at = pl.ds(pl.multiple_of(i * width, width), width)
            parts = pieces(qh[side, :, at])
            feats[side * leaves + i] = dot(parts.T.astype(BF16), src_sel[...]).astype(BF16)

    features(1)

    lane = lax.broadcasted_iota(jnp.int32, (rows_r, 128), 1)

    def to_rows(columns):
        held = jnp.zeros((rows_r, 128), F32)
        for k, column in enumerate(columns):
            held = jnp.where(lane == k, column, held)
        square[...] = jnp.zeros_like(square)
        square[0:rows_r, :] = held
        return square[...].T

    copies[2].wait()

    @pl.loop(0, rows_r // 8)
    def _(g):
        here = pl.ds(pl.multiple_of(g * 8, 8), 8)

        def add(c, sums):
            at = pl.ds(pl.multiple_of(c * 128, 128), 128)
            v = [kry[k, here, at] for k in range(krylov_len)]
            return tuple(s + v[k] * v[m] for s, (k, m) in zip(sums, pairs))

        sums = lax.fori_loop(
            0, leaves * width // 128, add, tuple(jnp.zeros((8, 128), F32) for _ in pairs), unroll=2)
        for t in range(len(pairs)):
            grams[t, here, :] = sums[t]

    def exchange(red, phase, level, block):
        count, own, peer_of = ((GROUP, low, group_peer), (lines, high, line_peer))[level]
        base = 2 * phase + level
        red[level, own] = block
        sent = [
            remote(red.at[level, own], red.at[level, own], peer_of(d), red_send.at[base, d], red_recv.at[base, d])
            for d in range(1, count)
        ]
        start(sent)

        def finish():
            wait(sent)
            total = red[level, 0]
            for d in range(1, count):
                total = total + red[level, d]
            return total

        return finish

    gram_rows = red_g.shape[2]
    block = to_rows([jnp.sum(grams[t], axis=1, keepdims=True) for t in range(len(pairs))])
    group_gram = exchange(red_g, 0, 0, block[0:gram_rows])

    for t in range(1, steps):
        highs[t - 1].wait()
        highs[t].start()
    for t in (0, 2, 1, 3):
        halos[t].wait()
    features(0)
    features(2)
    line_gram = exchange(red_g, 0, 1, group_gram())
    highs[-1].wait()
    start(first + side0)
    base_leaf = lax.axis_index("leaf") * leaves - leaves

    @pl.loop(0, leaves)
    def _(i):
        @pl.when(i == MARKS[0])
        def _():
            wait(first)
            start(second + side1)

        @pl.when(i == MARKS[1])
        def _():
            wait(second)
            start(side2)

        at = pl.ds(pl.multiple_of(i * width, width), width)
        parts = pieces(qh[1, :, at]).astype(BF16)
        weights = jnp.concatenate([dot(tgt_sel[0], parts), dot(tgt_sel[1], parts)], axis=1).astype(BF16)
        total = jnp.zeros((rows_r, width), F32)
        for j in range(near_ref.shape[1]):
            leaf = jnp.clip(near_ref[i, j] - base_leaf, 0, 3 * leaves - 1)
            both = dot(feats[leaf], weights)
            root = lax.rsqrt(both[:, :width])
            block = (both[:, width:] * (root * root * root)).astype(BF16)
            total += dot(dens[lax.div(leaf, leaves), lax.rem(leaf, leaves)], block)
        applied[:, at] = total

    wait(copies[3:])
    wait(side0 + side1 + side2)

    acc[...] = jnp.zeros_like(acc)

    @pl.loop(0, leaves, unroll=2)
    def _(i):
        at = pl.ds(pl.multiple_of(i * width, width), width)
        rows = []
        for k in range(far_dev.shape[1]):
            m = every[slot_of[far_dev[i, k]], far_local[i, k]]
            half = m.shape[1] // 2
            rows += [m[:, :half], m[:, half:]]
        local = dot(cp[i], jnp.concatenate(rows, axis=0)).astype(BF16).astype(F32)
        value = applied[:, at] + dot(local.T.astype(BF16), vb[i])
        applied[:, at] = value
        for k in range(krylov_len + 1):
            prod = value * (kry[k, :, at] if k < krylov_len else value)
            acc[k] += sum(prod[:, s:s + 128] for s in range(0, width, 128))

    part_rows = red_p.shape[2]
    block = to_rows([jnp.sum(acc[k], axis=1, keepdims=True) for k in range(krylov_len + 1)])
    group_part = exchange(red_p, 1, 0, block[0:part_rows])
    gram = line_gram()
    line_part = exchange(red_p, 1, 1, group_part())
    part = line_part()
    scale = 1.0 / npts
    inner_of = {}
    for t, (k, m) in enumerate(pairs):
        inner_of[k, m] = inner_of[m, k] = gram[t:t + 1] * scale
    with_a = [part[k:k + 1] * scale for k in range(krylov_len)]
    coeffs = [with_a[k] + 0.5 * inner_of[k, last] for k in range(krylov_len)]
    shifts = coeffs[:last] + [with_a[last] + 0.5 * (inner_of[last, last] - 1.0)]
    mean = part[krylov_len:krylov_len + 1] * scale
    for k in range(krylov_len):
        along = sum(shifts[m] * inner_of[k, m] for m in range(krylov_len))
        mean = mean + shifts[k] * (along - 2.0 * with_a[k])
    norm = jnp.sqrt(jnp.maximum(mean, 0.0) + EPSILON)
    square[...] = jnp.zeros_like(square)
    for k in range(krylov_len):
        square[k:k + 1, :] = shifts[k]
        square[16 + k:17 + k, :] = coeffs[k]
    hess_ref[0:krylov_len, :] = square[16:16 + krylov_len, 0:rows_r]
    hess_ref[krylov_len:krylov_len + 1, :] = norm[:, 0:rows_r]
    square[krylov_len:krylov_len + 1, :] = 1.0 / norm
    lanes = square[...].T[0:rows_r]
    inverse = jnp.broadcast_to(lanes[:, krylov_len:krylov_len + 1], (rows_r, 128))
    for k in range(krylov_len):
        acc[k] = jnp.broadcast_to(lanes[:, k:k + 1], (rows_r, 128)) * inverse
    acc[krylov_len] = inverse

    @pl.loop(0, leaves * width // 128)
    def _(i):
        at = pl.ds(pl.multiple_of(i * 128, 128), 128)
        value = applied[:, at] * acc[krylov_len]
        for k in range(krylov_len):
            value = value - acc[k] * kry[k, :, at]
        out_ref[:, at] = value


def shards(n, krylov_basis, geometry, near_leaf, far_dev, far_local, ubases, vbases, coupling):
    leaves, rank, width = ubases.shape
    krylov_len, columns, points = krylov_basis.shape
    bits = n.bit_length() - 1
    slot_of = np.array([int(format(d, f"0{bits}b")[::-1], 2) for d in range(n)], np.int32)
    src_sel, tgt_sel = selections()
    lines = n // GROUP
    pairs = krylov_len * (krylov_len + 1) // 2
    smem, vmem, hbm = (pl.BlockSpec(memory_space=s) for s in (pltpu.SMEM, pltpu.VMEM, pl.ANY))
    return pl.pallas_call(
        functools.partial(kernel, n, leaves, n * points),
        out_shape=(
            jax.ShapeDtypeStruct((krylov_len + 1, columns), F32),
            jax.ShapeDtypeStruct((columns, points), F32),
        ),
        in_specs=[smem, smem, smem, smem, vmem, vmem, vmem, hbm, hbm, hbm, hbm],
        out_specs=(vmem, vmem),
        scratch_shapes=[
            pltpu.VMEM(krylov_basis.shape, F32),
            pltpu.VMEM(ubases.shape, BF16),
            pltpu.VMEM(vbases.shape, BF16),
            pltpu.VMEM(coupling.shape, BF16),
            pltpu.VMEM((3, 8, points), F32),
            pltpu.VMEM((3, leaves, columns, width), BF16),
            pltpu.VMEM((3 * leaves, width, FEATURES), BF16),
            pltpu.VMEM((n, leaves, rank // 2, 2 * columns), BF16),
            pltpu.VMEM((columns, points), F32),
            pltpu.VMEM((pairs, columns, 128), F32),
            pltpu.VMEM((krylov_len + 1, columns, 128), F32),
            pltpu.VMEM((128, 128), F32),
            pltpu.VMEM((2, max(GROUP, lines), -(-pairs // 8) * 8, 128), F32),
            pltpu.VMEM((2, max(GROUP, lines), 16, 128), F32),
            pltpu.SemaphoreType.DMA((5,)),
            pltpu.SemaphoreType.DMA((4,)),
            pltpu.SemaphoreType.DMA((4,)),
            pltpu.SemaphoreType.DMA((bits + 8,)),
            pltpu.SemaphoreType.DMA((bits + 8,)),
            pltpu.SemaphoreType.DMA((4, max(GROUP, lines))),
            pltpu.SemaphoreType.DMA((4, max(GROUP, lines))),
        ],
        compiler_params=pltpu.CompilerParams(
            collective_id=0, has_side_effects=True, vmem_limit_bytes=56 * 1024 * 1024
        ),
    )(
        near_leaf, far_dev, far_local, jnp.asarray(slot_of), geometry, jnp.asarray(src_sel), jnp.asarray(tgt_sel),
        krylov_basis, ubases, vbases, coupling,
    )


def solution(mesh):
    in_specs = (
        P(None, None, ("groups", "leaf")),
        P(None, ("groups", "leaf")),
        P(("groups", "leaf"), None),
        P(("groups", "leaf"), None),
        P(("groups", "leaf"), None),
        P(("groups", "leaf"), None, None),
        P(("groups", "leaf"), None, None),
        P(("groups", "leaf"), None, None),
    )
    out_specs = (P("groups", None), P(None, ("groups", "leaf")))
    return jax.shard_map(
        functools.partial(shards, mesh.shape["leaf"]),
        mesh=mesh, in_specs=in_specs, out_specs=out_specs, check_vma=False,
    )
```

time: 124 us -> 80 us (0.65)
  Pallas kernels: 114 us -> 75.6 us
  other arithmetic: 4.44 us -> 0 us
    pallas_call x1, Pallas kernels: 114 us -> 75.6 us  [shards(): pl.pallas_call(functools.partial(kernel, n, leaves, n * points), out_shap...]
    add x3 -> x0, other arithmetic: 2.62 us -> none  [the longest x1 1.32 us: shards(): far_idx = reverse * leaves + far_local]
where the time goes in v2:
time: 80 us; the launch traced here: 79.8 us
  Pallas kernels  75.6 us (94%)
  local copies, waits for them, and re-layouts  3.57 us (4%)
    pallas_call x1, Pallas kernels, shards(): pl.pallas_call(functools.partial(kernel, n, leaves, n * points), out_shap...  75.6 us
    unnamed x2, local copies, waits for them, and re-layouts  3.57 us

profile of v2, /device:TPU:0, one launch (start us, length us, event | category | flops | bytes accessed | tf_op | source)
XLA Modules:
  0.0 79.8 jit_solution(1738855056957309794)
XLA Ops:
  0.6 75.6 %shard_map.122 = (f32[9,64]{1,0:T(8,128)}, f32[64,4096]{1,0:T(8,128)}) custom-call(s32[16,9]{1,0:T(8,128)} %near_ref.1, s32[16,16]{1,0:T(8,128)} %far_dev.1, s32[16,16]{1,0:T(8,128)} %far_local.1, s32[32]{0:T(128)} %constant.6.clone.slot_of, f32[7,4096]{1,0:T(8,128)} %geo_ref.1, bf16[32,48]{1,0:T(8,128)(2,1)} %constant.7.clone.src_sel, ...), custom_call_target="tpu_custom_call" | custom-call | tf_op jit(solution)/shard_map/pallas_call | solution.py:342
  76.2 1.3 %copy.15 = f32[9,64]{1,0:T(8,128)} copy(f32[9,64]{1,0:T(8,128)} %get-tuple-element.4) | data formatting | bytes 4608
  77.5 2.3 %copy.16 = f32[64,4096]{1,0:T(8,128)} copy(f32[64,4096]{1,0:T(8,128)} %get-tuple-element.5) | data formatting | bytes 2097152

commit v3 on v2

--- a/solution.py
+++ b/solution.py
@@ -88,8 +88,7 @@
         pltpu.make_async_copy(c_hbm, cp, in_sem.at[3]),
         pltpu.make_async_copy(v_hbm, vb, in_sem.at[4]),
     ]
-    for copy in copies:
-        copy.start()
+    copies[0].start()
 
     geo = geo_ref[...]
     x, normal, weight = geo[0:3], geo[3:6], geo[6:7]
@@ -107,6 +106,8 @@
     )
 
     copies[0].wait()
+    for copy in copies[1:]:
+        copy.start()
     for i in range(leaves):
         dens[1, i] = kry[last, :, i * width:(i + 1) * width].astype(BF16)
     pl.semaphore_wait(barrier, len(peers))

time: 80 us -> 80 us (level)
  no operation moved by 1% of the time
where the time goes in v3:
time: 80 us; the launch traced here: 79.7 us
  Pallas kernels  75.5 us (94%)
  local copies, waits for them, and re-layouts  3.57 us (4%)
    pallas_call x1, Pallas kernels, shards(): pl.pallas_call(functools.partial(kernel, n, leaves, n * points), out_shap...  75.5 us
    unnamed x2, local copies, waits for them, and re-layouts  3.57 us

profile of v3, /device:TPU:0, one launch (start us, length us, event | category | flops | bytes accessed | tf_op | source)
XLA Modules:
  0.0 79.7 jit_solution(12805243111201510913)
XLA Ops:
  0.6 75.5 %shard_map.122 = (f32[9,64]{1,0:T(8,128)}, f32[64,4096]{1,0:T(8,128)}) custom-call(s32[16,9]{1,0:T(8,128)} %near_ref.1, s32[16,16]{1,0:T(8,128)} %far_dev.1, s32[16,16]{1,0:T(8,128)} %far_local.1, s32[32]{0:T(128)} %constant.6.clone.slot_of, f32[7,4096]{1,0:T(8,128)} %geo_ref.1, bf16[32,48]{1,0:T(8,128)(2,1)} %constant.7.clone.src_sel, ...), custom_call_target="tpu_custom_call" | custom-call | tf_op jit(solution)/shard_map/pallas_call | solution.py:343
  76.2 1.3 %copy.15 = f32[9,64]{1,0:T(8,128)} copy(f32[9,64]{1,0:T(8,128)} %get-tuple-element.4) | data formatting | bytes 4608
  77.5 2.3 %copy.16 = f32[64,4096]{1,0:T(8,128)} copy(f32[64,4096]{1,0:T(8,128)} %get-tuple-element.5) | data formatting | bytes 2097152
